TPU v7x, 512 devices: a whole 4x8x8 slice. The times are simulated.
512 devices in a mesh: zt: 64 (over z, y), xy: 8 (over x, core).
Axes of the slice: x: 4, y: 8, z: 8, core: 2. Of those that a mesh axis runs over, the one named last changes fastest.
Arguments:
- right_side: float32 [8, 256, 96, 128], P('xy', 'zt'), may hold values from -200 to 200
- self_link: float32 [8, 256, 4, 4608], P('xy', 'zt'), may hold values from -1 to 4
- hop_links: float32 [8, 8, 256, 4, 4608], P(None, 'xy', 'zt'), may hold values from -0.3125 to 0.3125
Outputs:
- solution_field: float32 [8, 256, 96, 128], P('xy', 'zt')
- residual: float32 [8, 256, 96, 128], P('xy', 'zt')
All inputs are finite; a program needn't handle non-finite values.
Results may differ from a plain program's by a relative error of at most 0.00026.
Values sent between devices are 32-bit elements; how exact they have to be, the bound alone decides.
A program may use at most 128 MiB of HBM per device.

v0:
```python
import jax
import jax.numpy as jnp
from jax import lax
from jax.sharding import PartitionSpec as P

NV = 48
RHS = 32
NT = 32
NY = 4


HIGHEST = lax.Precision.HIGHEST


def extended(block, sides, width):
    for axis, dim in sides:
        count = lax.axis_size(axis)
        forward = [(i, i + 1) for i in range(count - 1)]
        forward.append((count - 1, 0))
        backward = [(target, source) for source, target in forward]
        low = lax.ppermute(
            lax.slice_in_dim(block, block.shape[dim] - width, None, axis=dim), axis, forward
        )
        high = lax.ppermute(lax.slice_in_dim(block, 0, width, axis=dim), axis, backward)
        block = jnp.concatenate([low, block, high], axis=dim)
    return block


def shifted(array, axis, by):
    count = lax.axis_size(axis)
    return lax.ppermute(array, axis, [(i, (i + by) % count) for i in range(count)])


def apply_link(packed, values):
    rows_x, rows_t = (values.shape[0], values.shape[1])
    links = packed.reshape(rows_x, rows_t, NY, 2, NV, NV)
    parts = values.reshape(rows_x, rows_t, 2, NV, NY, RHS)
    link_re = links[:, :, :, 0]
    link_im = links[:, :, :, 1]
    field_re = parts[:, :, 0]
    field_im = parts[:, :, 1]

    def product(matrix, vector):
        return jnp.einsum("xtyij,xtjyc->xtiyc", matrix, vector, precision=HIGHEST)

    new_re = product(link_re, field_re) - product(link_im, field_im)
    new_im = product(link_re, field_im) + product(link_im, field_re)
    return jnp.stack([new_re, new_im], axis=2).reshape(values.shape)


def operator(field, self_link, hop_links):
    rows_x, rows_t = (field.shape[0], field.shape[1])
    blocks = NT // rows_t
    padded_x = extended(field, (("xy", 0),), 1)
    padded_t = extended(field, (("zt", 1),), 1)
    z_above = shifted(field, "zt", -blocks)
    z_below = shifted(field, "zt", blocks)
    shaped = field.reshape(rows_x, rows_t, 2 * NV, NY, RHS)

    def flatten(values):
        return values.reshape(field.shape)

    summed = apply_link(self_link, field)
    summed = summed - apply_link(hop_links[0], padded_x[2:])
    summed = summed - apply_link(hop_links[1], padded_x[:-2])
    summed = summed - apply_link(hop_links[2], flatten(jnp.roll(shaped, -1, 3)))
    summed = summed - apply_link(hop_links[3], flatten(jnp.roll(shaped, 1, 3)))
    summed = summed - apply_link(hop_links[4], z_above)
    summed = summed - apply_link(hop_links[5], z_below)
    summed = summed - apply_link(hop_links[6], padded_t[:, 2:])
    summed = summed - apply_link(hop_links[7], padded_t[:, :-2])
    return summed


def complex_parts(field):
    shaped = field.reshape(field.shape[0], field.shape[1], 2, NV, NY, RHS)
    return (shaped[:, :, 0], shaped[:, :, 1])


def inner_local(left, right):
    left_re, left_im = complex_parts(left)
    right_re, right_im = complex_parts(right)

    def contract(first, second):
        return jnp.einsum("xtnsc,xtnsd->cd", first, second, precision=HIGHEST)

    return (
        contract(left_re, right_re) + contract(left_im, right_im),
        contract(left_re, right_im) - contract(left_im, right_re),
    )


def gram_solve(gram, target):
    gram_re, gram_im = gram
    target_re, target_im = target
    upper = jnp.concatenate([gram_re, -gram_im], axis=1)
    lower = jnp.concatenate([gram_im, gram_re], axis=1)
    matrix = jnp.concatenate([upper, lower], axis=0)
    matrix = 0.5 * (matrix + matrix.T)
    factor = jnp.linalg.cholesky(matrix)
    solved = jax.scipy.linalg.cho_solve(
        (factor, True), jnp.concatenate([target_re, target_im], axis=0)
    )
    count = gram_re.shape[0]
    return (solved[:count], solved[count:])


def combine(field, coef):
    coef_re, coef_im = coef
    field_re, field_im = complex_parts(field)

    def times(values, matrix):
        return jnp.einsum("xtnsc,cd->xtnsd", values, matrix, precision=HIGHEST)

    new_re = times(field_re, coef_re) - times(field_im, coef_im)
    new_im = times(field_re, coef_im) + times(field_im, coef_re)
    return jnp.stack([new_re, new_im], axis=2).reshape(field.shape)


def local(right_side, self_link, hop_links):
    first_image = operator(right_side, self_link, hop_links)
    gram_local = inner_local(first_image, first_image)
    target_local = inner_local(first_image, right_side)
    gram_re, gram_im, target_re, target_im = lax.psum(
        (gram_local[0], gram_local[1], target_local[0], target_local[1]), ("zt", "xy")
    )
    first_gram = (gram_re, gram_im)
    first_coef = gram_solve(first_gram, (target_re, target_im))
    residual_one = right_side - combine(first_image, first_coef)
    second_image = operator(residual_one, self_link, hop_links)
    correlation_local = inner_local(first_image, second_image)
    correlation_re, correlation_im = lax.psum(
        (correlation_local[0], correlation_local[1]), ("zt", "xy")
    )
    projection = gram_solve(first_gram, (correlation_re, correlation_im))
    direction_image = second_image - combine(first_image, projection)
    square_local = inner_local(direction_image, direction_image)
    aimed_local = inner_local(direction_image, residual_one)
    square_re, square_im, aimed_re, aimed_im = lax.psum(
        (square_local[0], square_local[1], aimed_local[0], aimed_local[1]), ("zt", "xy")
    )
    second_gram = (square_re, square_im)
    second_target = (aimed_re, aimed_im)
    direction = residual_one - combine(right_side, projection)
    second_coef = gram_solve(second_gram, second_target)
    solution_field = combine(right_side, first_coef) + combine(direction, second_coef)
    residual = residual_one - combine(direction_image, second_coef)
    return (solution_field, residual)


def solution(mesh):
    return jax.shard_map(
        local,
        mesh=mesh,
        in_specs=(
            P("xy", "zt", None, None),
            P("xy", "zt", None, None),
            P(None, "xy", "zt", None, None),
        ),
        out_specs=(P("xy", "zt", None, None), P("xy", "zt", None, None)),
        check_vma=False,
    )
```

profile of v0, /device:TPU:1, one launch (start us, length us, event | category | flops | bytes accessed | tf_op | source)
XLA Modules:
  0.0 592.2 jit_solution(17730164858686458114)
XLA Ops:
  0.6 11.5 %collective-permute-start.2 = (f32[1,4,96,128]{3,2,1,0:T(8,128)}, f32[1,4,96,128]{3,2,1,0:T(8,128)}, u32[]{:S(2)}, u32[]{:S(2)}) collective-permute-start(f32[1,4,96,128]{3,2,1,0:T(8,128)} %param.6), channel_id=1, source_target_pairs={{0,448},{8,456},{16,464},{24,472},{32,480},{40,488},{48,496},{56,5... | collective-permute-start | bytes 589832 | tf_op jit(solution)/shard_map/ppermute | solution.py:31
  12.1 2.1 collective-permute-start.1
  15.7 3.2 collective-permute-start.5
  18.9 5.4 collective-permute-start.4
  45.5 2.2 reshape_squeeze.39
  47.7 2.2 reshape_squeeze.37
  60.7 2.2 reshape.1624
  72.3 2.5 fusion.30
  80.6 2.2 reshape.1623
  87.4 2.2 reshape.1620
  92.8 2.2 reshape.1621
  100.8 2.2 reshape.1622
  117.2 10.7 %fusion.37 = f32[1,4,1,48,4,32]{3,5,4,1,2,0:T(8,128)S(1)} fusion(f32[4,4,32,48]{3,2,1,0:T(8,128)S(1)} %fusion.95, f32[1,4,4,2,48,48]{5,4,3,2,1,0:T(8,128)S(1)} %reshape_squeeze.36, f32[1,4,1,48,4,32]{3,5,4,1,2,0:T(8,128)S(1)} %copy-done.47), kind=kOutput, calls=%fused_computation.75 | convolution fusion | flops 14180352 | bytes 1015808 | tf_op jit(solution)/shard_map/xtyij,xtjyc->xtiyc/dot_general | solution.py:44
  137.6 97.3 %all-reduce.2 = (f32[32,32]{1,0:T(8,128)S(1)}, f32[32,32]{1,0:T(8,128)S(1)}, f32[32,32]{1,0:T(8,128)S(1)}, f32[32,32]{1,0:T(8,128)S(1)}) all-reduce(f32[32,32]{1,0:T(8,128)S(1)} %fusion.51, f32[32,32]{1,0:T(8,128)S(1)} %fusion.50, f32[32,32]{1,0:T(8,128)S(1)} %fusion.48, ...), channel_id=1, replica_groups=mesh['zt'=64,'xy'=8] {'zt','xy'}, use_global_device_ids=true, to_apply=%region_5.7 | all-reduce | flops 4096 | bytes 32768 | tf_op jit(solution)/shard_map/psum | solution.py:124
  235.3 5.8 cholesky.44
  242.5 4.9 custom-call.9
  260.2 4.6 collective-permute-start.8
  264.7 2.5 collective-permute-start.7
  270.5 2.1 reshape.1558
  276.6 7.1 %collective-permute-start.10 = (f32[1,1,96,128]{2,3,1,0:T(8,128)}, f32[1,1,96,128]{2,3,1,0:T(8,128)}, u32[]{:S(2)}, u32[]{:S(2)}) collective-permute-start(f32[1,1,96,128]{2,3,1,0:T(8,128)} %get-tuple-element.73), channel_id=1, source_target_pairs={{8,0},{16,8},{24,16},{32,24},{40,32},{48,40},{56,48},{64,56},{72,6... | collective-permute-start | bytes 147464 | tf_op jit(solution)/shard_map/ppermute | solution.py:24
  285.4 2.1 reshape_reshape.14
  296.5 2.1 reshape_reshape.15
  315.0 2.1 reshape.1581
  325.4 2.1 reshape.1578
  335.6 2.1 reshape.1575
  345.9 2.1 reshape.1572
  354.1 2.1 reshape.1564
  370.1 94.5 %all-reduce.1 = (f32[32,32]{1,0:T(8,128)S(1)}, f32[32,32]{1,0:T(8,128)S(1)}) all-reduce(f32[32,32]{1,0:T(8,128)S(1)} %fusion.53, f32[32,32]{1,0:T(8,128)S(1)} %fusion.52), channel_id=1, replica_groups=mesh['zt'=64,'xy'=8] {'zt','xy'}, use_global_device_ids=true, to_apply=%region_7.10 | all-reduce | flops 2048 | bytes 16384 | tf_op jit(solution)/shard_map/psum | solution.py:132
  468.9 2.4 maximum_subtract_fusion.2
  474.4 94.8 %all-reduce = (f32[32,32]{1,0:T(8,128)S(1)}, f32[32,32]{1,0:T(8,128)S(1)}, f32[32,32]{1,0:T(8,128)S(1)}, f32[32,32]{1,0:T(8,128)S(1)}) all-reduce(f32[32,32]{1,0:T(8,128)S(1)} %fusion.57, f32[32,32]{1,0:T(8,128)S(1)} %fusion.56, f32[32,32]{1,0:T(8,128)S(1)} %fusion.54, ...), channel_id=1, replica_groups=mesh['zt'=64,'xy'=8] {'zt','xy'}, use_global_device_ids=true, to_apply=%region_11.14 | all-reduce | flops 4096 | bytes 32768 | tf_op jit(solution)/shard_map/psum | solution.py:139
  569.5 5.8 cholesky.55
  576.6 4.9 custom-call.11
  (368 shorter events, 197.2 us)
Async XLA Ops:
  0.6 100.1 %collective-permute-start.2 = (f32[1,4,96,128]{3,2,1,0:T(8,128)}, f32[1,4,96,128]{3,2,1,0:T(8,128)}, u32[]{:S(2)}, u32[]{:S(2)}) collective-permute-start(f32[1,4,96,128]{3,2,1,0:T(8,128)} %param.6), channel_id=1, source_target_pairs={{0,448},{8,456},{16,464},{24,472},{32,480},{40,488},{48,496},{56,5... | collective-permute-start | bytes 589832 | tf_op jit(solution)/shard_map/ppermute | solution.py:31
  12.1 80.7 %collective-permute-start.1 = (f32[1,4,96,128]{3,2,1,0:T(8,128)}, f32[1,4,96,128]{3,2,1,0:T(8,128)}, u32[]{:S(2)}, u32[]{:S(2)}) collective-permute-start(f32[1,4,96,128]{3,2,1,0:T(8,128)} %param.6), channel_id=1, source_target_pairs={{0,1},{1,2},{2,3},{3,4},{4,5},{5,6},{6,7},{7,0},{8,9},{9,10},{10,1... | collective-permute-start | bytes 589832 | tf_op jit(solution)/shard_map/ppermute | solution.py:21
  14.2 73.2 %collective-permute-start = (f32[1,4,96,128]{3,2,1,0:T(8,128)}, f32[1,4,96,128]{3,2,1,0:T(8,128)}, u32[]{:S(2)}, u32[]{:S(2)}) collective-permute-start(f32[1,4,96,128]{3,2,1,0:T(8,128)} %param.6), channel_id=1, source_target_pairs={{1,0},{2,1},{3,2},{4,3},{5,4},{6,5},{7,6},{0,7},{9,8},{10,9},{11,1... | collective-permute-start | bytes 589832 | tf_op jit(solution)/shard_map/ppermute | solution.py:24
  15.7 36.9 %collective-permute-start.5 = (f32[1,1,96,128]{3,2,1,0:T(8,128)}, f32[1,1,96,128]{3,2,1,0:T(8,128)}, u32[]{:S(2)}, u32[]{:S(2)}) collective-permute-start(f32[1,1,96,128]{3,2,1,0:T(8,128)} %get-tuple-element.84), channel_id=1, source_target_pairs={{0,8},{8,16},{16,24},{24,32},{32,40},{40,48},{48,56},{56,64},{64,7... | collective-permute-start | bytes 147464 | tf_op jit(solution)/shard_map/ppermute | solution.py:21
  18.9 35.6 %collective-permute-start.4 = (f32[1,1,96,128]{3,2,1,0:T(8,128)S(1)}, f32[1,1,96,128]{3,2,1,0:T(8,128)}, u32[]{:S(2)}, u32[]{:S(2)}) collective-permute-start(f32[1,1,96,128]{3,2,1,0:T(8,128)S(1)} %get-tuple-element.85), channel_id=1, source_target_pairs={{8,0},{16,8},{24,16},{32,24},{40,32},{48,40},{56,48},{64,56},{72,6... | collective-permute-start | bytes 147464 | tf_op jit(solution)/shard_map/ppermute | solution.py:24
  28.5 5.6 copy-start.4
  35.4 5.7 copy-start.8
  41.1 6.6 %copy-start.10 = (f32[1,4,4,2,48,48]{5,4,3,2,1,0:T(8,128)}, f32[1,4,4,2,48,48]{5,4,3,2,1,0:T(8,128)S(1)}, u32[]{:S(2)}) copy-start(f32[1,4,4,2,48,48]{5,4,3,2,1,0:T(8,128)S(1)} %reshape_squeeze.34) | copy-start | bytes 884740
  42.6 7.3 %copy-start.50 = (f32[1,1,4,4,4608]{4,3,2,1,0:T(4,128)S(1)}, f32[1,1,4,4,4608]{4,3,2,1,0:T(4,128)}, u32[]{:S(2)}) copy-start(f32[1,1,4,4,4608]{4,3,2,1,0:T(4,128)} %get-tuple-element.18) | copy-start | bytes 884740
  44.1 6.2 %copy-start.49 = (f32[1,1,4,4,4608]{4,3,2,1,0:T(4,128)S(1)}, f32[1,1,4,4,4608]{4,3,2,1,0:T(4,128)}, u32[]{:S(2)}) copy-start(f32[1,1,4,4,4608]{4,3,2,1,0:T(4,128)} %get-tuple-element.21) | copy-start | bytes 884740
  52.6 28.0 %collective-permute-start.3 = (f32[1,4,96,128]{3,2,1,0:T(8,128)}, f32[1,4,96,128]{3,2,1,0:T(8,128)}, u32[]{:S(2)}, u32[]{:S(2)}) collective-permute-start(f32[1,4,96,128]{3,2,1,0:T(8,128)} %param.6), channel_id=1, source_target_pairs={{0,64},{8,72},{16,80},{24,88},{32,96},{40,104},{48,112},{56,120},{... | collective-permute-start | bytes 589832 | tf_op jit(solution)/shard_map/ppermute | solution.py:31
  68.7 6.1 %copy-start.6 = (f32[1,4,4,2,48,48]{5,4,3,2,1,0:T(8,128)S(1)}, f32[1,4,4,2,48,48]{5,4,3,2,1,0:T(8,128)}, u32[]{:S(2)}) copy-start(f32[1,4,4,2,48,48]{5,4,3,2,1,0:T(8,128)} %reshape_squeeze.39) | copy-start | bytes 884740
  68.7 7.5 %copy-start.2 = (f32[1,4,4,2,48,48]{5,4,3,2,1,0:T(8,128)S(1)}, f32[1,4,4,2,48,48]{5,4,3,2,1,0:T(8,128)}, u32[]{:S(2)}) copy-start(f32[1,4,4,2,48,48]{5,4,3,2,1,0:T(8,128)} %reshape_squeeze.38) | copy-start | bytes 884740
  68.7 7.5 %copy-start.45 = (f32[1,4,1,48,4,32]{3,5,4,1,2,0:T(8,128)S(1)}, f32[1,4,1,48,4,32]{3,5,4,1,2,0:T(8,128)}, u32[]{:S(2)}) copy-start(f32[1,4,1,48,4,32]{3,5,4,1,2,0:T(8,128)} %copy.192) | copy-start | bytes 294916
  68.7 8.3 %copy-start.44 = (f32[1,4,1,48,4,32]{3,5,4,1,2,0:T(8,128)S(1)}, f32[1,4,1,48,4,32]{3,5,4,1,2,0:T(8,128)}, u32[]{:S(2)}) copy-start(f32[1,4,1,48,4,32]{3,5,4,1,2,0:T(8,128)} %copy.190) | copy-start | bytes 294916
  108.7 5.6 copy-start
  108.7 5.6 copy-start.41
  108.7 6.3 %copy-start.47 = (f32[1,4,1,48,4,32]{3,5,4,1,2,0:T(8,128)S(1)}, f32[1,4,1,48,4,32]{3,5,4,1,2,0:T(8,128)}, u32[]{:S(2)}) copy-start(f32[1,4,1,48,4,32]{3,5,4,1,2,0:T(8,128)} %copy.182) | copy-start | bytes 294916
  108.7 7.1 %copy-start.46 = (f32[1,4,1,48,4,32]{3,5,4,1,2,0:T(8,128)S(1)}, f32[1,4,1,48,4,32]{3,5,4,1,2,0:T(8,128)}, u32[]{:S(2)}) copy-start(f32[1,4,1,48,4,32]{3,5,4,1,2,0:T(8,128)} %copy.184) | copy-start | bytes 294916
  115.0 12.9 %copy-start.43 = (f32[1,4,1,48,4,32]{3,5,4,1,2,0:T(8,128)S(1)}, f32[1,4,1,48,4,32]{3,5,4,1,2,0:T(8,128)}, u32[]{:S(2)}) copy-start(f32[1,4,1,48,4,32]{3,5,4,1,2,0:T(8,128)} %copy.170) | copy-start | bytes 294916
  115.0 13.6 %copy-start.42 = (f32[1,4,1,48,4,32]{3,5,4,1,2,0:T(8,128)S(1)}, f32[1,4,1,48,4,32]{3,5,4,1,2,0:T(8,128)}, u32[]{:S(2)}) copy-start(f32[1,4,1,48,4,32]{3,5,4,1,2,0:T(8,128)} %copy.172) | copy-start | bytes 294916
  258.2 77.4 %collective-permute-start.9 = (f32[1,4,96,128]{2,3,1,0:T(8,128)}, f32[1,4,96,128]{2,3,1,0:T(8,128)}, u32[]{:S(2)}, u32[]{:S(2)}) collective-permute-start(f32[1,4,96,128]{2,3,1,0:T(8,128)} %sub.500), channel_id=1, source_target_pairs={{0,64},{8,72},{16,80},{24,88},{32,96},{40,104},{48,112},{56,120},{... | collective-permute-start | bytes 589832 | tf_op jit(solution)/shard_map/ppermute | solution.py:31
  260.2 85.7 %collective-permute-start.8 = (f32[1,4,96,128]{2,3,1,0:T(8,128)}, f32[1,4,96,128]{2,3,1,0:T(8,128)}, u32[]{:S(2)}, u32[]{:S(2)}) collective-permute-start(f32[1,4,96,128]{2,3,1,0:T(8,128)} %sub.500), channel_id=1, source_target_pairs={{0,448},{8,456},{16,464},{24,472},{32,480},{40,488},{48,496},{56,5... | collective-permute-start | bytes 589832 | tf_op jit(solution)/shard_map/ppermute | solution.py:31
  264.7 89.4 %collective-permute-start.7 = (f32[1,4,96,128]{2,3,1,0:T(8,128)}, f32[1,4,96,128]{2,3,1,0:T(8,128)}, u32[]{:S(2)}, u32[]{:S(2)}) collective-permute-start(f32[1,4,96,128]{2,3,1,0:T(8,128)} %sub.500), channel_id=1, source_target_pairs={{0,1},{1,2},{2,3},{3,4},{4,5},{5,6},{6,7},{7,0},{8,9},{9,10},{10,1... | collective-permute-start | bytes 589832 | tf_op jit(solution)/shard_map/ppermute | solution.py:21
  274.6 38.4 %collective-permute-start.11 = (f32[1,1,96,128]{2,3,1,0:T(8,128)}, f32[1,1,96,128]{2,3,1,0:T(8,128)}, u32[]{:S(2)}, u32[]{:S(2)}) collective-permute-start(f32[1,1,96,128]{2,3,1,0:T(8,128)} %get-tuple-element.72), channel_id=1, source_target_pairs={{0,8},{8,16},{16,24},{24,32},{32,40},{40,48},{48,56},{56,64},{64,7... | collective-permute-start | bytes 147464 | tf_op jit(solution)/shard_map/ppermute | solution.py:21
  276.6 36.5 %collective-permute-start.10 = (f32[1,1,96,128]{2,3,1,0:T(8,128)}, f32[1,1,96,128]{2,3,1,0:T(8,128)}, u32[]{:S(2)}, u32[]{:S(2)}) collective-permute-start(f32[1,1,96,128]{2,3,1,0:T(8,128)} %get-tuple-element.73), channel_id=1, source_target_pairs={{8,0},{16,8},{24,16},{32,24},{40,32},{48,40},{56,48},{64,56},{72,6... | collective-permute-start | bytes 147464 | tf_op jit(solution)/shard_map/ppermute | solution.py:24
  289.3 6.4 %copy-start.66 = (f32[1,4,96,3,32]{2,4,3,1,0:T(8,128)S(1)}, f32[1,4,96,3,32]{2,4,3,1,0:T(8,128)}, u32[]{:S(2)}) copy-start(f32[1,4,96,3,32]{2,4,3,1,0:T(8,128)} %get-tuple-element.76) | copy-start | bytes 442372
  300.4 6.5 %copy-start.48 = (f32[1,4,2,48,4,32]{3,2,5,4,1,0:T(2,128)S(1)}, f32[1,4,2,48,4,32]{3,2,5,4,1,0:T(2,128)}, u32[]{:S(2)}) copy-start(f32[1,4,2,48,4,32]{3,2,5,4,1,0:T(2,128)} %reshape.1558) | copy-start | bytes 589828
  313.0 49.5 %collective-permute-start.6 = (f32[1,4,96,128]{2,3,1,0:T(8,128)}, f32[1,4,96,128]{2,3,1,0:T(8,128)}, u32[]{:S(2)}, u32[]{:S(2)}) collective-permute-start(f32[1,4,96,128]{2,3,1,0:T(8,128)} %sub.500), channel_id=1, source_target_pairs={{1,0},{2,1},{3,2},{4,3},{5,4},{6,5},{7,6},{0,7},{9,8},{10,9},{11,1... | collective-permute-start | bytes 589832 | tf_op jit(solution)/shard_map/ppermute | solution.py:24
  369.7 99.1 %copy-start.28 = (f32[1,4,1,48,4,32]{3,5,4,1,2,0:T(8,128)S(1)}, f32[1,4,1,48,4,32]{3,5,4,1,2,0:T(8,128)}, u32[]{:S(2)}) copy-start(f32[1,4,1,48,4,32]{3,5,4,1,2,0:T(8,128)} %fusion.8) | copy-start | bytes 294916
  472.1 110.7 %copy-start.53 = (f32[32,4,48,4]{2,0,3,1:T(8,128)S(1)}, f32[32,4,48,4]{2,0,3,1:T(8,128)}, u32[]{:S(2)}) copy-start(f32[32,4,48,4]{2,0,3,1:T(8,128)} %fusion.200) | copy-start | bytes 294916
  472.9 110.4 %copy-start.52 = (f32[32,4,48,4]{2,0,3,1:T(8,128)S(1)}, f32[32,4,48,4]{2,0,3,1:T(8,128)}, u32[]{:S(2)}) copy-start(f32[32,4,48,4]{2,0,3,1:T(8,128)} %fusion.202) | copy-start | bytes 294916
  (48 other events, 157.1 us)
where the time goes:
time: 603 us; the launch traced here: 592 us
  blocking collectives  287 us (48%)
  matrix products  121 us (20%)
  local copies, waits for them, and re-layouts  102 us (17%)
  starting transfers between devices  42.1 us (7%)
  other arithmetic  37.2 us (6%)
    dot_general x72, matrix products, product(): return jnp.einsum('xtyij,xtjyc->xtiyc', matrix, vector, precision=HIGHEST)  97.9 us
    psum x1, blocking collectives, local(): lax.psum((gram_local[0], gram_local[1], target_local[0], target_local[1])...  97.3 us
    psum x1, blocking collectives, local(): lax.psum((square_local[0], square_local[1], aimed_local[0], aimed_local[1...  94.8 us
    psum x1, blocking collectives, local(): lax.psum((correlation_local[0], correlation_local[1]), ('zt', 'xy'))  94.5 us
    reshape x13, local copies, waits for them, and re-layouts, apply_link(): parts = values.reshape(rows_x, rows_t, 2, NV, NY, RHS)  25.8 us
    unnamed x152, local copies, waits for them, and re-layouts  20.4 us
    ppermute x4, starting transfers between devices, shifted(): lax.ppermute(array, axis, [(i, (i + by) % count) for i in range(count)])  19.9 us
    dot_general x24, matrix products, times(): return jnp.einsum('xtnsc,cd->xtnsd', values, matrix, precision=HIGHEST)  14.5 us
  transfers between devices with their start and end apart: 12, of which 0 were waited for; matrix products, arithmetic and copies ran while one was open for 27% of the time, Pallas kernels for 0%

commit v1 on v0

v1 whole, which is shorter than its diff:
```python
import functools

import jax
import jax.numpy as jnp
from jax import lax
from jax.experimental import pallas as pl
from jax.experimental.pallas import tpu as pltpu
from jax.sharding import PartitionSpec as P

NV = 48
RHS = 32
NT = 32
NY = 4
ROWS = 4

MESH = pl.DeviceIdType.MESH
HIGHEST = lax.Precision.HIGHEST
F32 = jnp.float32
BF16 = jnp.bfloat16

HOP_OF_SLOT = (None, 2, 3, 6, 7, 0, 1, 4, 5)
SLOTS = 9
KSLOT = 256


def dot(left, right):
    return jnp.dot(left, right, precision=HIGHEST, preferred_element_type=F32)


def lane_iota(rows):
    return lax.broadcasted_iota(jnp.int32, (rows, 128), 1)


def times_minus_i(rows):
    half = rows.shape[0] // 2
    return jnp.concatenate([rows[half:], -rows[:half]], axis=0)


def field_rows(ref, first=0):
    return ref[first : first + ROWS].reshape(ROWS * 2 * NV, 128)


def field_j(rows):
    parts = []
    for t in range(ROWS):
        base = t * 2 * NV
        parts.append(rows[base + NV : base + 2 * NV])
        parts.append(-rows[base : base + NV])
    return jnp.concatenate(parts, axis=0)


def diagonal_sum(product, tile, group):
    total = None
    for y in range(NY):
        block = product[32 * y : 32 * (y + 1), 128 * tile : 128 * (tile + 1)]
        shift = (32 * (group - y)) % 128
        if shift:
            block = pltpu.roll(block, shift, 1)
        total = block if total is None else total + block
    return total


def by_group(group, parts):
    out = parts[-1]
    for index in range(len(parts) - 2, -1, -1):
        out = jnp.where(group == index, parts[index], out)
    return out


def packed_inner(product, tiles):
    group = lane_iota(32) // 32
    return by_group(group, [diagonal_sum(product, tile, g) for g, tile in enumerate(tiles)])


def eliminate(packed):
    group = lane_iota(32) // 32
    lane = lane_iota(32)
    row32 = lax.broadcasted_iota(jnp.int32, (32, 128), 0)
    eye = jnp.where(lane == row32 + 96, 1.0, 0.0).astype(F32)
    down = pltpu.roll(packed, 96, 1)
    up = pltpu.roll(packed, 32, 1)
    top = by_group(group, [packed, -packed, packed, eye])
    bottom = by_group(group, [down, up, down, jnp.zeros_like(packed)])
    work = jnp.concatenate([top, bottom], axis=0)
    row = lax.broadcasted_iota(jnp.int32, (64, 128), 0)
    for k in range(RHS):
        inverse = 1.0 / work[k : k + 1, k : k + 1]
        first = work[k : k + 1, :] * inverse
        second = work[k + 32 : k + 33, :] * inverse
        updated = work - work[:, k : k + 1] * first - work[:, k + 32 : k + 33] * second
        work = jnp.where(row == k, first, jnp.where(row == k + 32, second, updated))
    return work


def repeated(block, group_index):
    group = lane_iota(32) // 32
    block = jnp.where(group == group_index, block, 0.0)
    block = block + pltpu.roll(block, 64, 1)
    return block + pltpu.roll(block, 32, 1)


def column_matrix(coef, group_index):
    group = lane_iota(32) // 32
    real = repeated(coef[:32], group_index)
    imag = repeated(coef[32:], group_index)
    blocks = [jnp.where(group == y, real, 0.0) for y in range(NY)]
    blocks += [jnp.where(group == y, -imag, 0.0) for y in range(NY)]
    return jnp.concatenate(blocks, axis=0)


def kernel(
    sizes,
    b_ref,
    self_ref,
    hop_ref,
    sol_ref,
    res_ref,
    raw,
    rows_scr,
    amat,
    bhi,
    blo,
    ext,
    halo,
    acc,
    second,
    first_res,
    pay,
    rs_buf,
    z_buf,
    x_buf,
    ag_buf,
    link_sem,
    b_sem,
    halo_send,
    halo_recv,
    t_send,
    t_recv,
    red_send,
    red_recv,
):
    yb, zb, xb = sizes
    zt = lax.axis_index("zt")
    xy = lax.axis_index("xy")
    my_y = lax.rem(zt, yb)
    my_z = lax.div(zt, yb)
    count = yb * zb

    def zt_at(by):
        return lax.rem(zt + (by + count), count)

    def xy_at(by):
        return lax.rem(xy + (by + xb), xb)

    def link_copies(slot):
        source = self_ref.at[0] if slot == 0 else hop_ref.at[HOP_OF_SLOT[slot], 0]
        return pltpu.make_async_copy(source, raw.at[slot], link_sem.at[slot])

    own = pltpu.make_async_copy(b_ref.at[0], ext.at[0, pl.ds(1, ROWS)], b_sem)
    own.start()
    for slot in range(SLOTS):
        link_copies(slot).start()

    partners = [(zt_at(1), xy), (zt_at(-1), xy)]
    partners += [(my_z * yb + lax.rem(my_y + o, yb), xy) for o in range(1, yb)]
    partners += [(lax.rem(my_z + o, zb) * yb + my_y, xy) for o in range(1, zb)]
    partners += [(zt, lax.rem(xy + o, xb)) for o in range(1, xb)]
    barrier = pltpu.get_barrier_semaphore()
    for partner in partners:
        pl.semaphore_signal(barrier, inc=1, device_id=partner, device_id_type=MESH)
    pl.semaphore_wait(barrier, len(partners))

    targets = ((zt, xy_at(-1)), (zt, xy_at(1)), (zt_at(-yb), xy), (zt_at(yb), xy))

    def halo_copy(which, side, t):
        return pltpu.make_async_remote_copy(
            src_ref=ext.at[which, 1 + t],
            dst_ref=halo.at[which, side, t],
            send_sem=halo_send.at[which, side, t],
            recv_sem=halo_recv.at[which, side, t],
            device_id=targets[side],
            device_id_type=MESH,
        )

    def t_copy(which, side):
        return pltpu.make_async_remote_copy(
            src_ref=ext.at[which, 1 if side == 0 else ROWS],
            dst_ref=ext.at[which, ROWS + 1 if side == 0 else 0],
            send_sem=t_send.at[which, side],
            recv_sem=t_recv.at[which, side],
            device_id=(zt_at(-1) if side == 0 else zt_at(1), xy),
            device_id_type=MESH,
        )

    own.wait()
    t_copy(0, 0).start()
    t_copy(0, 1).start()

    def start_b(t, carry):
        for side in (2, 3, 0, 1):
            halo_copy(0, side, t).start()
        return carry

    lax.fori_loop(0, ROWS, start_b, 0)

    bhi[...] = jnp.zeros_like(bhi)
    blo[...] = jnp.zeros_like(blo)
    for slot in range(SLOTS):
        link_copies(slot).wait()
    lane = lane_iota(8)
    odd = lax.rem(lax.broadcasted_iota(jnp.int32, (8, 128), 0), 2) == 1

    def relayout(step, carry):
        slot = lax.div(step, 2)
        pair = lax.rem(step, 2)
        for g in range(12):
            tiles = [
                raw[slot, pl.ds(2 * pair, 2), :, 384 * g + 128 * n : 384 * g + 128 * (n + 1)].reshape(8, 128)
                for n in range(3)
            ]
            turned = [pltpu.roll(tile, 64, 1) for tile in tiles]
            tiles = [
                jnp.where(odd, jnp.where(lane < 64, turned[n - 1], turned[n]), tiles[n]) for n in range(3)
            ]
            for r in range(8):
                n, offset = divmod(48 * r, 128)
                piece = tiles[n]
                if offset:
                    piece = jnp.where(lane < offset, tiles[(n + 1) % 3], piece)
                    piece = pltpu.roll(piece, 128 - offset, 1)
                rows_scr[pl.ds(8 * g + r, 8, stride=96), :] = piece
        low = lane_iota(96) < 64
        for t in range(2):
            for h in range(2):
                base = (t * 4 + 2 * h) * 96
                values = jnp.where(low, rows_scr[base : base + 96, :], rows_scr[base + 96 : base + 192, :])
                hi = values.astype(BF16)
                lo = (values - hi.astype(F32)).astype(BF16)
                amat[2 * pair + t, slot, 0:96, 128 * h : 128 * (h + 1)] = hi
                amat[2 * pair + t, slot, 96:192, 128 * h : 128 * (h + 1)] = lo
        return carry

    lax.fori_loop(0, 2 * SLOTS, relayout, 0)

    group48 = lane_iota(48) // 32

    def put(slot, real, imag):
        for half, part in ((0, real), (1, imag)):
            hi = part.astype(BF16).astype(F32)
            lo = part - hi
            for y in range(NY):
                mask = group48 == y
                at = slice(slot * KSLOT + 64 * y, slot * KSLOT + 64 * y + 48)
                lanes = slice(128 * half, 128 * (half + 1))
                bhi[at, lanes] = jnp.where(mask, hi, 0.0).astype(BF16)
                blo[at, lanes] = jnp.where(mask, lo, 0.0).astype(BF16)

    def put_site(slot, site):
        put(slot, site[0:NV], site[NV : 2 * NV])

    def product(t, first, last):
        left = jnp.concatenate([amat[t, s] for s in range(first, last)], axis=1)
        right = slice(first * KSLOT, last * KSLOT)
        main = jnp.dot(left, bhi[right, :], preferred_element_type=F32)
        rest = jnp.dot(left[0:96], blo[right, :], preferred_element_type=F32)
        return main[0:96] + main[96:192] + rest

    def near(which):
        def body(t, carry):
            site = ext[which, 1 + t]
            put_site(0, -site)
            put_site(1, pltpu.roll(site, 96, 1))
            put_site(2, pltpu.roll(site, 32, 1))
            acc[t] = product(t, 0, 3)
            return carry

        lax.fori_loop(0, ROWS, body, 0)

    def far(which, out):
        t_copy(which, 0).wait_recv()
        t_copy(which, 1).wait_recv()

        def body(t, carry):
            for side in range(4):
                halo_copy(which, side, t).wait_recv()
            put_site(3, ext[which, 2 + t])
            put_site(4, ext[which, t])
            for side in range(4):
                put_site(5 + side, halo[which, side, t])
            total = acc[t] + product(t, 3, SLOTS)
            real = total[48:96, 128:256] - total[0:48, 0:128]
            imag = -(total[48:96, 0:128] + total[0:48, 128:256])
            out(t, real, imag)
            return carry

        lax.fori_loop(0, ROWS, body, 0)

    def image_out(t, real, imag):
        ext[1, 1 + t, 0:NV, :] = real
        ext[1, 1 + t, NV : 2 * NV, :] = imag
        for side in (2, 3, 0, 1):
            halo_copy(1, side, t).start()

    near(0)
    far(0, image_out)
    t_copy(1, 0).start()
    t_copy(1, 1).start()

    piece = 64 // yb

    def exchange(red, phase, buffer, me, size, source, device):
        def copy(o):
            return pltpu.make_async_remote_copy(
                src_ref=source(lax.rem(me + o, size)),
                dst_ref=buffer.at[red, me],
                send_sem=red_send.at[red, phase, o],
                recv_sem=red_recv.at[red, phase, me],
                device_id=device(lax.rem(me + o, size)),
                device_id_type=MESH,
            )

        def arrival(o):
            other = lax.rem(me + o, size)
            return pltpu.make_async_remote_copy(
                src_ref=source(other),
                dst_ref=buffer.at[red, other],
                send_sem=red_send.at[red, phase, o],
                recv_sem=red_recv.at[red, phase, other],
                device_id=device(other),
                device_id_type=MESH,
            )

        def start():
            for o in range(1, size):
                copy(o).start()

        def wait():
            for o in range(1, size):
                arrival(o).wait_recv()

        def drain():
            for o in range(1, size):
                copy(o).wait_send()

        return start, wait, drain

    def y_device(other):
        return (my_z * yb + other, xy)

    def z_device(other):
        return (other * yb + my_y, xy)

    def x_device(other):
        return (zt, other)

    def reduction(red):
        scatter = exchange(red, 0, rs_buf, my_y, yb, lambda other: pay.at[red, other], y_device)
        along_z = exchange(red, 1, z_buf, my_z, zb, lambda other: z_buf.at[red, my_z], z_device)
        along_x = exchange(red, 2, x_buf, xy, xb, lambda other: x_buf.at[red, xy], x_device)
        gather = exchange(red, 3, ag_buf, my_y, yb, lambda other: ag_buf.at[red, my_y], y_device)

        def summed(buffer, size):
            total = buffer[red, 0]
            for n in range(1, size):
                total = total + buffer[red, n]
            return total

        def step0(values):
            for n in range(yb):
                pay[red, n] = values[n * piece : (n + 1) * piece]
            rs_buf[red, my_y] = pay[red, my_y]
            scatter[0]()

        def step1():
            scatter[1]()
            z_buf[red, my_z] = summed(rs_buf, yb)
            along_z[0]()

        def step2():
            along_z[1]()
            x_buf[red, xy] = summed(z_buf, zb)
            along_x[0]()

        def step3():
            along_x[1]()
            ag_buf[red, my_y] = summed(x_buf, xb)
            gather[0]()

        def step4():
            gather[1]()
            return jnp.concatenate([ag_buf[red, n] for n in range(yb)], axis=0)

        def drain():
            for part in (scatter, along_z, along_x, gather):
                part[2]()

        return step0, step1, step2, step3, step4, drain

    red1 = reduction(0)
    red2 = reduction(1)

    rhs_rows = field_rows(ext.at[0], 1)
    image_rows = field_rows(ext.at[1], 1)
    columns = jnp.concatenate([image_rows, field_j(image_rows), rhs_rows, field_j(rhs_rows)], axis=1)
    inner = dot(image_rows.T, columns)
    packed = packed_inner(inner, (0, 1, 2, 3))
    red1[0](jnp.concatenate([packed, jnp.zeros_like(packed)], axis=0))

    near(1)
    red1[1]()

    def twice_out(t, real, imag):
        second[t, 0:NV, :] = real
        second[t, NV : 2 * NV, :] = imag

    red1[2]()
    far(1, twice_out)
    red1[3]()
    gram = red1[4]()[0:32]
    solved = eliminate(gram)

    coef1 = column_matrix(solved, 2)
    image_rows = field_rows(ext.at[1], 1)
    image_j = field_j(image_rows)
    residual_rows = field_rows(ext.at[0], 1) - dot(jnp.concatenate([image_rows, image_j], axis=1), coef1)
    twice_rows = field_rows(second)
    second_rows = image_rows - dot(jnp.concatenate([twice_rows, field_j(twice_rows)], axis=1), coef1)
    first_res[...] = residual_rows.reshape(ROWS, 2 * NV, 128)
    second[...] = second_rows.reshape(ROWS, 2 * NV, 128)

    columns = jnp.concatenate(
        [second_rows, field_j(second_rows), residual_rows, field_j(residual_rows)], axis=1
    )
    with_image = dot(image_rows.T, columns)
    with_second = dot(second_rows.T, columns)
    group = lane_iota(32) // 32
    first_pack = packed_inner(with_image, (0, 1, 2, 3))
    second_pack = packed_inner(with_second, (0, 1, 2, 3))
    red2[0](
        jnp.concatenate(
            [
                jnp.where(group < 2, first_pack, second_pack),
                jnp.where(group < 2, second_pack, first_pack),
            ],
            axis=0,
        )
    )

    zero32 = jnp.zeros((32, 128), F32)

    def real_form(real, imag):
        top = by_group(group, [real, -pltpu.roll(imag, 32, 1), zero32, zero32])
        bottom = by_group(group, [imag, pltpu.roll(real, 32, 1), zero32, zero32])
        return jnp.concatenate([top, bottom], axis=0)

    gram_form = real_form(gram, pltpu.roll(gram, 96, 1))
    inverse_form = real_form(pltpu.roll(solved[:32], 32, 1), pltpu.roll(solved[32:], 32, 1))

    def times(form, stacked):
        return dot(form[:, 0:64], stacked)

    red2[1]()
    red2[2]()
    red2[3]()
    reduced = red2[4]()
    upper, lower = reduced[:32], reduced[32:]
    group64 = lane_iota(64) // 32
    cross = jnp.where(group64 == 0, jnp.concatenate([upper, pltpu.roll(upper, 96, 1)], axis=0), 0.0)
    aside = jnp.where(
        group64 == 0, jnp.concatenate([pltpu.roll(lower, 64, 1), pltpu.roll(lower, 32, 1)], axis=0), 0.0
    )
    projection = times(inverse_form, cross)
    excess = times(gram_form, projection) - cross
    left = projection + pltpu.roll(cross, 32, 1)
    right = jnp.concatenate(
        [
            excess
            + pltpu.roll(times_minus_i(excess), 32, 1)
            + pltpu.roll(aside, 64, 1)
            + pltpu.roll(times_minus_i(aside), 96, 1),
            projection + pltpu.roll(times_minus_i(projection), 32, 1),
        ],
        axis=1,
    )
    inner = dot(left.T, right)
    packed = jnp.where(
        group < 2,
        lower - inner[32:64, 128:256] + inner[0:32, 0:128],
        upper - inner[0:32, 0:128],
    )
    solved2 = eliminate(packed)

    projection_form = real_form(projection[:32], projection[32:])
    follow = times(projection_form, solved2)
    coef2 = column_matrix(solved2, 2)
    coef_follow = column_matrix(follow, 2)
    coef_right = column_matrix(solved - follow, 2)
    rhs_rows = field_rows(ext.at[0], 1)
    image_rows = field_rows(ext.at[1], 1)
    residual_rows = field_rows(first_res)
    second_rows = field_rows(second)
    answer = dot(
        jnp.concatenate([rhs_rows, field_j(rhs_rows), residual_rows, field_j(residual_rows)], axis=1),
        jnp.concatenate([coef_right, coef2], axis=0),
    )
    sol_ref[0] = answer.reshape(ROWS, 2 * NV, 128)
    change = dot(
        jnp.concatenate([second_rows, field_j(second_rows), image_rows, field_j(image_rows)], axis=1),
        jnp.concatenate([-coef2, coef_follow], axis=0),
    )
    res_ref[0] = (residual_rows + change).reshape(ROWS, 2 * NV, 128)

    for which in range(2):
        t_copy(which, 0).wait_send()
        t_copy(which, 1).wait_send()

    def drain(t, carry):
        for which in range(2):
            for side in range(4):
                halo_copy(which, side, t).wait_send()
        return carry

    lax.fori_loop(0, ROWS, drain, 0)
    red1[5]()
    red2[5]()


def solution(mesh):
    yb = NT // ROWS
    zb = mesh.shape["zt"] // yb
    xb = mesh.shape["xy"]
    piece = 64 // yb
    block = jax.ShapeDtypeStruct((1, ROWS, 2 * NV, 128), F32)

    def local(right_side, self_link, hop_links):
        any_space = pl.BlockSpec(memory_space=pl.ANY)
        in_vmem = pl.BlockSpec(memory_space=pltpu.VMEM)
        return pl.pallas_call(
            functools.partial(kernel, (yb, zb, xb)),
            out_shape=(block, block),
            in_specs=[any_space, any_space, any_space],
            out_specs=(in_vmem, in_vmem),
            scratch_shapes=[
                pltpu.VMEM((SLOTS, ROWS, NY, 2 * NV * NV), F32),
                pltpu.VMEM((8 * 96, 128), F32),
                pltpu.VMEM((ROWS, SLOTS, 192, KSLOT), BF16),
                pltpu.VMEM((SLOTS * KSLOT, 256), BF16),
                pltpu.VMEM((SLOTS * KSLOT, 256), BF16),
                pltpu.VMEM((2, ROWS + 2, 2 * NV, 128), F32),
                pltpu.VMEM((2, 4, ROWS, 2 * NV, 128), F32),
                pltpu.VMEM((ROWS, 96, 256), F32),
                pltpu.VMEM((ROWS, 2 * NV, 128), F32),
                pltpu.VMEM((ROWS, 2 * NV, 128), F32),
                pltpu.VMEM((2, yb, piece, 128), F32),
                pltpu.VMEM((2, yb, piece, 128), F32),
                pltpu.VMEM((2, zb, piece, 128), F32),
                pltpu.VMEM((2, xb, piece, 128), F32),
                pltpu.VMEM((2, yb, piece, 128), F32),
                pltpu.SemaphoreType.DMA((SLOTS,)),
                pltpu.SemaphoreType.DMA,
                pltpu.SemaphoreType.DMA((2, 4, ROWS)),
                pltpu.SemaphoreType.DMA((2, 4, ROWS)),
                pltpu.SemaphoreType.DMA((2, 2)),
                pltpu.SemaphoreType.DMA((2, 2)),
                pltpu.SemaphoreType.DMA((2, 4, 8)),
                pltpu.SemaphoreType.DMA((2, 4, 8)),
            ],
            compiler_params=pltpu.CompilerParams(
                collective_id=0, has_side_effects=True, vmem_limit_bytes=48 * 1024 * 1024
            ),
            name="two_gcr_iterations",
        )(right_side, self_link, hop_links)

    return jax.shard_map(
        local,
        mesh=mesh,
        in_specs=(
            P("xy", "zt", None, None),
            P("xy", "zt", None, None),
            P(None, "xy", "zt", None, None),
        ),
        out_specs=(P("xy", "zt", None, None), P("xy", "zt", None, None)),
        check_vma=False,
    )
```

time: 603 us -> 79.3 us (0.13); the launches traced: 592 us -> 79.1 us
  blocking collectives: 287 us -> 0 us
  matrix products: 121 us -> 0 us
  local copies, waits for them, and re-layouts: 102 us -> 4.9 us
  Pallas kernels: 0 us -> 73.5 us
  starting transfers between devices: 42.1 us -> 0 us
  other arithmetic: 37.2 us -> 0 us
    psum x3 -> x0, blocking collectives: 287 us -> none  [the longest x1 97.3 us: local(): lax.psum((gram_local[0], gram_local[1], target_local[0], target_local[1])...]
    dot_general x116 -> x0, matrix products: 120 us -> none  [the longest x72 97.9 us: product(): return jnp.einsum('xtyij,xtjyc->xtiyc', matrix, vector, precision=HIGHEST)]
    pallas_call x0 -> x1, Pallas kernels: none -> 73.5 us  [local(): pl.pallas_call(functools.partial(kernel, (yb, zb, xb)), out_shape=(block,...]
    ppermute x12 -> x0, starting transfers between devices: 42.1 us -> none  [the longest x4 19.9 us: shifted(): lax.ppermute(array, axis, [(i, (i + by) % count) for i in range(count)])]
    slice x26 -> x0, local copies, waits for them, and re-layouts: 35.3 us -> none  [the longest x9 14.4 us: apply_link(): field_im = parts[:, :, 1]]
    reshape x19 -> x0, local copies, waits for them, and re-layouts: 29.5 us -> none  [the longest x13 25.8 us: apply_link(): parts = values.reshape(rows_x, rows_t, 2, NV, NY, RHS)]
    another operation x13 -> x0, other arithmetic: 24.3 us -> none  [the longest x6 13 us: gram_solve(): factor = jnp.linalg.cholesky(matrix)]
    another operation x18 -> x0, local copies, waits for them, and re-layouts: 16.6 us -> none  [the longest x8 9.66 us: apply_link(): links = packed.reshape(rows_x, rows_t, NY, 2, NV, NV)]
  transfers between devices with their start and end apart: 12 -> 0, of which waited for: 0 -> 0; matrix products, arithmetic and copies ran while one was open for 27% -> 0% of each run, Pallas kernels for 0% -> 0%
where the time goes in v1:
time: 79.3 us; the launch traced here: 79.1 us
  Pallas kernels  73.5 us (93%)
  local copies, waits for them, and re-layouts  4.9 us (6%)
    pallas_call x1, Pallas kernels, local(): pl.pallas_call(functools.partial(kernel, (yb, zb, xb)), out_shape=(block,...  73.5 us
    unnamed x8, local copies, waits for them, and re-layouts  4.9 us

profile of v1, /device:TPU:1, one launch (start us, length us, event | category | flops | bytes accessed | tf_op | source)
XLA Modules:
  0.0 79.1 jit_solution(14687732264281116881)
XLA Ops:
  0.6 0.0 copy-start
  0.6 1.7 %copy-done = f32[8,1,4,4,4608]{4,3,2,1,0:T(4,128)S(1)} copy-done((f32[8,1,4,4,4608]{4,3,2,1,0:T(4,128)S(1)}, f32[8,1,4,4,4608]{4,3,2,1,0:T(4,128)}, u32[]{:S(2)}) %copy-start) | copy-done | bytes 2359320
  2.3 0.0 copy-start.1
  2.3 1.0 %copy-done.1 = f32[1,4,4,4608]{3,2,1,0:T(4,128)S(1)} copy-done((f32[1,4,4,4608]{3,2,1,0:T(4,128)S(1)}, f32[1,4,4,4608]{3,2,1,0:T(4,128)}, u32[]{:S(2)}) %copy-start.1) | copy-done | bytes 294936
  3.3 0.0 copy-start.2
  3.3 0.9 %copy-done.2 = f32[1,4,96,128]{3,2,1,0:T(8,128)S(1)} copy-done((f32[1,4,96,128]{3,2,1,0:T(8,128)S(1)}, f32[1,4,96,128]{3,2,1,0:T(8,128)}, u32[]{:S(2)}) %copy-start.2) | copy-done | bytes 196632
  4.2 73.5 %two_gcr_iterations.1 = (f32[1,4,96,128]{3,2,1,0:T(8,128)S(1)}, f32[1,4,96,128]{3,2,1,0:T(8,128)S(1)}) custom-call(f32[1,4,96,128]{3,2,1,0:T(8,128)S(1)} %copy-done.2, f32[1,4,4,4608]{3,2,1,0:T(4,128)S(1)} %copy-done.1, f32[8,1,4,4,4608]{4,3,2,1,0:T(4,128)S(1)} %copy-done), custom_call_target="tpu_custom_call" | custom-call | tf_op jit(solution)/shard_map/two_gcr_iterations/pallas_call | solution.py:538
  77.7 0.7 copy.7
  78.4 0.7 copy.8
Async XLA Ops:
  0.6 1.7 %copy-start = (f32[8,1,4,4,4608]{4,3,2,1,0:T(4,128)S(1)}, f32[8,1,4,4,4608]{4,3,2,1,0:T(4,128)}, u32[]{:S(2)}) copy-start(f32[8,1,4,4,4608]{4,3,2,1,0:T(4,128)} %hop_ref.1) | copy-start | bytes 7077892
  2.3 1.0 %copy-start.1 = (f32[1,4,4,4608]{3,2,1,0:T(4,128)S(1)}, f32[1,4,4,4608]{3,2,1,0:T(4,128)}, u32[]{:S(2)}) copy-start(f32[1,4,4,4608]{3,2,1,0:T(4,128)} %self_ref.1) | copy-start | bytes 884740
  3.3 0.9 %copy-start.2 = (f32[1,4,96,128]{3,2,1,0:T(8,128)S(1)}, f32[1,4,96,128]{3,2,1,0:T(8,128)}, u32[]{:S(2)}) copy-start(f32[1,4,96,128]{3,2,1,0:T(8,128)} %b_ref.1) | copy-start | bytes 589828

commit v2 on v1

--- a/solution.py
+++ b/solution.py
@@ -124,11 +124,10 @@
     halo,
     acc,
     second,
-    first_res,
     pay,
     rs_buf,
+    y_buf,
     z_buf,
-    x_buf,
     ag_buf,
     link_sem,
     b_sem,
@@ -306,7 +305,7 @@
     t_copy(1, 0).start()
     t_copy(1, 1).start()
 
-    piece = 64 // yb
+    piece = 64 // xb
 
     def exchange(red, phase, buffer, me, size, source, device):
         def copy(o):
@@ -354,10 +353,10 @@
         return (zt, other)
 
     def reduction(red):
-        scatter = exchange(red, 0, rs_buf, my_y, yb, lambda other: pay.at[red, other], y_device)
-        along_z = exchange(red, 1, z_buf, my_z, zb, lambda other: z_buf.at[red, my_z], z_device)
-        along_x = exchange(red, 2, x_buf, xy, xb, lambda other: x_buf.at[red, xy], x_device)
-        gather = exchange(red, 3, ag_buf, my_y, yb, lambda other: ag_buf.at[red, my_y], y_device)
+        scatter = exchange(red, 0, rs_buf, xy, xb, lambda other: pay.at[red, other], x_device)
+        along_y = exchange(red, 1, y_buf, my_y, yb, lambda other: y_buf.at[red, my_y], y_device)
+        along_z = exchange(red, 2, z_buf, my_z, zb, lambda other: z_buf.at[red, my_z], z_device)
+        gather = exchange(red, 3, ag_buf, xy, xb, lambda other: ag_buf.at[red, xy], x_device)
 
         def summed(buffer, size):
             total = buffer[red, 0]
@@ -366,45 +365,49 @@
             return total
 
         def step0(values):
-            for n in range(yb):
+            for n in range(xb):
                 pay[red, n] = values[n * piece : (n + 1) * piece]
-            rs_buf[red, my_y] = pay[red, my_y]
+            rs_buf[red, xy] = pay[red, xy]
             scatter[0]()
 
         def step1():
             scatter[1]()
-            z_buf[red, my_z] = summed(rs_buf, yb)
+            y_buf[red, my_y] = summed(rs_buf, xb)
+            along_y[0]()
+
+        def step2():
+            along_y[1]()
+            z_buf[red, my_z] = summed(y_buf, yb)
             along_z[0]()
 
-        def step2():
+        def step3():
             along_z[1]()
-            x_buf[red, xy] = summed(z_buf, zb)
-            along_x[0]()
-
-        def step3():
-            along_x[1]()
-            ag_buf[red, my_y] = summed(x_buf, xb)
+            ag_buf[red, xy] = summed(z_buf, zb)
             gather[0]()
 
         def step4():
             gather[1]()
-            return jnp.concatenate([ag_buf[red, n] for n in range(yb)], axis=0)
+            return jnp.concatenate([ag_buf[red, n] for n in range(xb)], axis=0)
 
         def drain():
-            for part in (scatter, along_z, along_x, gather):
+            for part in (scatter, along_y, along_z, gather):
                 part[2]()
 
         return step0, step1, step2, step3, step4, drain
 
     red1 = reduction(0)
     red2 = reduction(1)
+    group = lane_iota(32) // 32
+    group64 = lane_iota(64) // 32
+    zero32 = jnp.zeros((32, 128), F32)
 
     rhs_rows = field_rows(ext.at[0], 1)
+    rhs_pair = jnp.concatenate([rhs_rows, field_j(rhs_rows)], axis=1)
     image_rows = field_rows(ext.at[1], 1)
-    columns = jnp.concatenate([image_rows, field_j(image_rows), rhs_rows, field_j(rhs_rows)], axis=1)
-    inner = dot(image_rows.T, columns)
+    image_pair = jnp.concatenate([image_rows, field_j(image_rows)], axis=1)
+    inner = dot(image_rows.T, jnp.concatenate([image_pair, rhs_pair], axis=1))
     packed = packed_inner(inner, (0, 1, 2, 3))
-    red1[0](jnp.concatenate([packed, jnp.zeros_like(packed)], axis=0))
+    red1[0](jnp.concatenate([packed, zero32], axis=0))
 
     near(1)
     red1[1]()
@@ -413,102 +416,86 @@
         second[t, 0:NV, :] = real
         second[t, NV : 2 * NV, :] = imag
 
-    red1[2]()
     far(1, twice_out)
-    red1[3]()
-    gram = red1[4]()[0:32]
-    solved = eliminate(gram)
-
-    coef1 = column_matrix(solved, 2)
+
+    rhs_rows = field_rows(ext.at[0], 1)
+    rhs_pair = jnp.concatenate([rhs_rows, field_j(rhs_rows)], axis=1)
     image_rows = field_rows(ext.at[1], 1)
-    image_j = field_j(image_rows)
-    residual_rows = field_rows(ext.at[0], 1) - dot(jnp.concatenate([image_rows, image_j], axis=1), coef1)
+    image_pair = jnp.concatenate([image_rows, field_j(image_rows)], axis=1)
     twice_rows = field_rows(second)
-    second_rows = image_rows - dot(jnp.concatenate([twice_rows, field_j(twice_rows)], axis=1), coef1)
-    first_res[...] = residual_rows.reshape(ROWS, 2 * NV, 128)
-    second[...] = second_rows.reshape(ROWS, 2 * NV, 128)
-
-    columns = jnp.concatenate(
-        [second_rows, field_j(second_rows), residual_rows, field_j(residual_rows)], axis=1
-    )
-    with_image = dot(image_rows.T, columns)
-    with_second = dot(second_rows.T, columns)
-    group = lane_iota(32) // 32
-    first_pack = packed_inner(with_image, (0, 1, 2, 3))
-    second_pack = packed_inner(with_second, (0, 1, 2, 3))
+    twice_pair = jnp.concatenate([twice_rows, field_j(twice_rows)], axis=1)
+    with_image = dot(image_rows.T, twice_pair)
+    with_twice = dot(twice_rows.T, jnp.concatenate([image_pair, twice_pair, rhs_pair], axis=1))
+    with_both = jnp.concatenate([with_image, with_twice[:, 0:256]], axis=1)
     red2[0](
         jnp.concatenate(
-            [
-                jnp.where(group < 2, first_pack, second_pack),
-                jnp.where(group < 2, second_pack, first_pack),
-            ],
-            axis=0,
+            [packed_inner(with_both, (0, 1, 2, 3)), packed_inner(with_twice, (2, 3, 4, 5))], axis=0
         )
     )
-
-    zero32 = jnp.zeros((32, 128), F32)
 
     def real_form(real, imag):
         top = by_group(group, [real, -pltpu.roll(imag, 32, 1), zero32, zero32])
         bottom = by_group(group, [imag, pltpu.roll(real, 32, 1), zero32, zero32])
         return jnp.concatenate([top, bottom], axis=0)
 
-    gram_form = real_form(gram, pltpu.roll(gram, 96, 1))
-    inverse_form = real_form(pltpu.roll(solved[:32], 32, 1), pltpu.roll(solved[32:], 32, 1))
-
-    def times(form, stacked):
-        return dot(form[:, 0:64], stacked)
-
+    def stacked(packed, first):
+        turns = [pltpu.roll(packed, (128 - 32 * g) % 128, 1) if g else packed for g in (first, first + 1)]
+        return jnp.where(group64 == 0, jnp.concatenate(turns, axis=0), 0.0)
+
+    def form_of(column):
+        return real_form(column[:32], column[32:])
+
+    red1[2]()
     red2[1]()
+    red1[3]()
     red2[2]()
+    gram = red1[4]()[0:32]
+    solved = eliminate(gram)
+    gram_column = stacked(gram, 0)
+    gram_form = form_of(gram_column)
+    target_column = stacked(gram, 2)
+    coef1 = jnp.where(group64 == 0, pltpu.roll(solved, 64, 1), 0.0)
+    inverse_form = form_of(pltpu.roll(solved, 32, 1))
+    coef1_form = form_of(coef1)
     red2[3]()
     reduced = red2[4]()
     upper, lower = reduced[:32], reduced[32:]
-    group64 = lane_iota(64) // 32
-    cross = jnp.where(group64 == 0, jnp.concatenate([upper, pltpu.roll(upper, 96, 1)], axis=0), 0.0)
-    aside = jnp.where(
-        group64 == 0, jnp.concatenate([pltpu.roll(lower, 64, 1), pltpu.roll(lower, 32, 1)], axis=0), 0.0
+
+    cross_form = form_of(stacked(upper, 0))
+    image_part = gram_column - dot(cross_form[:, 0:64], coef1)
+    projection = dot(inverse_form[:, 0:64], image_part)
+    row64 = lax.broadcasted_iota(jnp.int32, (64, 128), 0)
+    identity = jnp.where(lane_iota(64) == row64, jnp.where(group64 == 0, 1.0, 0.0), 0.0).astype(F32)
+    keep = identity - projection
+
+    grams = jnp.concatenate(
+        [
+            gram_form + pltpu.roll(cross_form, 64, 1),
+            form_of(stacked(upper, 2)) + pltpu.roll(form_of(stacked(lower, 0)), 64, 1),
+        ],
+        axis=0,
     )
-    projection = times(inverse_form, cross)
-    excess = times(gram_form, projection) - cross
-    left = projection + pltpu.roll(cross, 32, 1)
-    right = jnp.concatenate(
-        [
-            excess
-            + pltpu.roll(times_minus_i(excess), 32, 1)
-            + pltpu.roll(aside, 64, 1)
-            + pltpu.roll(times_minus_i(aside), 96, 1),
-            projection + pltpu.roll(times_minus_i(projection), 32, 1),
-        ],
-        axis=1,
-    )
-    inner = dot(left.T, right)
-    packed = jnp.where(
-        group < 2,
-        lower - inner[32:64, 128:256] + inner[0:32, 0:128],
-        upper - inner[0:32, 0:128],
-    )
-    solved2 = eliminate(packed)
-
-    projection_form = real_form(projection[:32], projection[32:])
-    follow = times(projection_form, solved2)
-    coef2 = column_matrix(solved2, 2)
-    coef_follow = column_matrix(follow, 2)
-    coef_right = column_matrix(solved - follow, 2)
+    weights = jnp.concatenate([keep, -coef1], axis=0)
+    applied = dot(grams, weights - jnp.concatenate([pltpu.roll(coef1, 64, 1), jnp.zeros_like(coef1)], axis=0))
+    targets12 = jnp.concatenate([target_column, stacked(lower, 2)], axis=0)
+    applied = applied + pltpu.roll(targets12, 64, 1)
+    turned = jnp.concatenate([times_minus_i(applied[:64]), times_minus_i(applied[64:])], axis=0)
+    applied = applied + pltpu.roll(turned, 32, 1)
+    solved2 = eliminate(dot(weights.T, applied)[0:32])
+
+    follow = dot(jnp.concatenate([form_of(keep), coef1_form], axis=0)[:, 0:64], solved2)
+    step_a = column_matrix(pltpu.roll(coef1, 64, 1) + follow[:64], 2)
+    step_e = column_matrix(follow[64:], 2)
     rhs_rows = field_rows(ext.at[0], 1)
+    rhs_pair = jnp.concatenate([rhs_rows, field_j(rhs_rows)], axis=1)
     image_rows = field_rows(ext.at[1], 1)
-    residual_rows = field_rows(first_res)
-    second_rows = field_rows(second)
-    answer = dot(
-        jnp.concatenate([rhs_rows, field_j(rhs_rows), residual_rows, field_j(residual_rows)], axis=1),
-        jnp.concatenate([coef_right, coef2], axis=0),
-    )
+    image_pair = jnp.concatenate([image_rows, field_j(image_rows)], axis=1)
+    twice_rows = field_rows(second)
+    twice_pair = jnp.concatenate([twice_rows, field_j(twice_rows)], axis=1)
+    answer = dot(jnp.concatenate([rhs_pair, image_pair], axis=1), jnp.concatenate([step_a, -step_e], axis=0))
     sol_ref[0] = answer.reshape(ROWS, 2 * NV, 128)
-    change = dot(
-        jnp.concatenate([second_rows, field_j(second_rows), image_rows, field_j(image_rows)], axis=1),
-        jnp.concatenate([-coef2, coef_follow], axis=0),
-    )
-    res_ref[0] = (residual_rows + change).reshape(ROWS, 2 * NV, 128)
+    change = dot(jnp.concatenate([image_pair, twice_pair], axis=1), jnp.concatenate([-step_a, step_e], axis=0))
+    res_ref[0] = (rhs_rows + change).reshape(ROWS, 2 * NV, 128)
 
     for which in range(2):
         t_copy(which, 0).wait_send()
@@ -529,16 +516,16 @@
     yb = NT // ROWS
     zb = mesh.shape["zt"] // yb
     xb = mesh.shape["xy"]
-    piece = 64 // yb
+    piece = 64 // xb
     block = jax.ShapeDtypeStruct((1, ROWS, 2 * NV, 128), F32)
 
     def local(right_side, self_link, hop_links):
-        any_space = pl.BlockSpec(memory_space=pl.ANY)
+        in_hbm = pl.BlockSpec(memory_space=pltpu.HBM)
         in_vmem = pl.BlockSpec(memory_space=pltpu.VMEM)
         return pl.pallas_call(
             functools.partial(kernel, (yb, zb, xb)),
             out_shape=(block, block),
-            in_specs=[any_space, any_space, any_space],
+            in_specs=[in_hbm, in_hbm, in_hbm],
             out_specs=(in_vmem, in_vmem),
             scratch_shapes=[
                 pltpu.VMEM((SLOTS, ROWS, NY, 2 * NV * NV), F32),
@@ -550,12 +537,11 @@
                 pltpu.VMEM((2, 4, ROWS, 2 * NV, 128), F32),
                 pltpu.VMEM((ROWS, 96, 256), F32),
                 pltpu.VMEM((ROWS, 2 * NV, 128), F32),
-                pltpu.VMEM((ROWS, 2 * NV, 128), F32),
-                pltpu.VMEM((2, yb, piece, 128), F32),
+                pltpu.VMEM((2, xb, piece, 128), F32),
+                pltpu.VMEM((2, xb, piece, 128), F32),
                 pltpu.VMEM((2, yb, piece, 128), F32),
                 pltpu.VMEM((2, zb, piece, 128), F32),
                 pltpu.VMEM((2, xb, piece, 128), F32),
-                pltpu.VMEM((2, yb, piece, 128), F32),
                 pltpu.SemaphoreType.DMA((SLOTS,)),
                 pltpu.SemaphoreType.DMA,
                 pltpu.SemaphoreType.DMA((2, 4, ROWS)),
@@ -569,7 +555,7 @@
                 collective_id=0, has_side_effects=True, vmem_limit_bytes=48 * 1024 * 1024
             ),
             name="two_gcr_iterations",
-        )(right_side, self_link, hop_links)
+        )(*[pltpu.with_memory_space_constraint(x, pltpu.HBM) for x in (right_side, self_link, hop_links)])
 
     return jax.shard_map(
         local,

time: 79.3 us -> 59.6 us (0.75)
  Pallas kernels: 73.5 us -> 57.5 us
  local copies, waits for them, and re-layouts: 4.9 us -> 1.36 us
    pallas_call x1, Pallas kernels: 73.5 us -> 57.5 us  [local(): pl.pallas_call(functools.partial(kernel, (yb, zb, xb)), out_shape=(block,...]
    unnamed x8 -> x2, local copies, waits for them, and re-layouts: 4.9 us -> 1.36 us
where the time goes in v2:
time: 59.6 us; the launch traced here: 59.4 us
  Pallas kernels  57.5 us (96%)
  local copies, waits for them, and re-layouts  1.36 us (2%)
  between operations  0.64 us (1%)
    pallas_call x1, Pallas kernels, local(): pl.pallas_call(functools.partial(kernel, (yb, zb, xb)), out_shape=(block,...  57.5 us
    unnamed x2, local copies, waits for them, and re-layouts  1.36 us

profile of v2, /device:TPU:1, one launch (start us, length us, event | category | flops | bytes accessed | tf_op | source)
XLA Modules:
  0.0 59.4 jit_solution(9372431186996732324)
XLA Ops:
  0.6 57.5 %two_gcr_iterations.1 = (f32[1,4,96,128]{3,2,1,0:T(8,128)S(1)}, f32[1,4,96,128]{3,2,1,0:T(8,128)S(1)}) custom-call(f32[1,4,96,128]{3,2,1,0:T(8,128)} %b_ref.1, f32[1,4,4,4608]{3,2,1,0:T(4,128)} %self_ref.1, f32[8,1,4,4,4608]{4,3,2,1,0:T(4,128)} %hop_ref.1), custom_call_target="tpu_custom_call" | custom-call | tf_op jit(solution)/shard_map/two_gcr_iterations/pallas_call | solution.py:525
  58.1 0.7 %copy.7 = f32[1,4,96,128]{3,2,1,0:T(8,128)} copy(f32[1,4,96,128]{3,2,1,0:T(8,128)S(1)} %get-tuple-element.4) | data formatting | bytes 393216
  58.8 0.7 %copy.8 = f32[1,4,96,128]{3,2,1,0:T(8,128)} copy(f32[1,4,96,128]{3,2,1,0:T(8,128)S(1)} %get-tuple-element.5) | data formatting | bytes 393216

commit v3 on v2

--- a/solution.py
+++ b/solution.py
@@ -21,6 +21,7 @@
 HOP_OF_SLOT = (None, 2, 3, 6, 7, 0, 1, 4, 5)
 SLOTS = 9
 KSLOT = 256
+PITCH = 97
 
 
 def dot(left, right):
@@ -227,12 +228,12 @@
                 if offset:
                     piece = jnp.where(lane < offset, tiles[(n + 1) % 3], piece)
                     piece = pltpu.roll(piece, 128 - offset, 1)
-                rows_scr[pl.ds(8 * g + r, 8, stride=96), :] = piece
+                rows_scr[pl.ds(8 * g + r, 8, stride=PITCH), :] = piece
         low = lane_iota(96) < 64
         for t in range(2):
             for h in range(2):
-                base = (t * 4 + 2 * h) * 96
-                values = jnp.where(low, rows_scr[base : base + 96, :], rows_scr[base + 96 : base + 192, :])
+                base = (t * 4 + 2 * h) * PITCH
+                values = jnp.where(low, rows_scr[base : base + 96, :], rows_scr[base + PITCH : base + PITCH + 96, :])
                 hi = values.astype(BF16)
                 lo = (values - hi.astype(F32)).astype(BF16)
                 amat[2 * pair + t, slot, 0:96, 128 * h : 128 * (h + 1)] = hi
@@ -264,12 +265,15 @@
         rest = jnp.dot(left[0:96], blo[right, :], preferred_element_type=F32)
         return main[0:96] + main[96:192] + rest
 
+    def near_sites(site):
+        put_site(0, -site)
+        put_site(1, pltpu.roll(site, 96, 1))
+        put_site(2, pltpu.roll(site, 32, 1))
+
     def near(which):
         def body(t, carry):
             site = ext[which, 1 + t]
-            put_site(0, -site)
-            put_site(1, pltpu.roll(site, 96, 1))
-            put_site(2, pltpu.roll(site, 32, 1))
+            near_sites(site)
             acc[t] = product(t, 0, 3)
             return carry
 
@@ -286,7 +290,11 @@
             put_site(4, ext[which, t])
             for side in range(4):
                 put_site(5 + side, halo[which, side, t])
-            total = acc[t] + product(t, 3, SLOTS)
+            if which:
+                total = acc[t] + product(t, 3, SLOTS)
+            else:
+                near_sites(ext[which, 1 + t])
+                total = product(t, 0, SLOTS)
             real = total[48:96, 128:256] - total[0:48, 0:128]
             imag = -(total[48:96, 0:128] + total[0:48, 128:256])
             out(t, real, imag)
@@ -300,7 +308,6 @@
         for side in (2, 3, 0, 1):
             halo_copy(1, side, t).start()
 
-    near(0)
     far(0, image_out)
     t_copy(1, 0).start()
     t_copy(1, 1).start()
@@ -529,7 +536,7 @@
             out_specs=(in_vmem, in_vmem),
             scratch_shapes=[
                 pltpu.VMEM((SLOTS, ROWS, NY, 2 * NV * NV), F32),
-                pltpu.VMEM((8 * 96, 128), F32),
+                pltpu.VMEM((8 * PITCH, 128), F32),
                 pltpu.VMEM((ROWS, SLOTS, 192, KSLOT), BF16),
                 pltpu.VMEM((SLOTS * KSLOT, 256), BF16),
                 pltpu.VMEM((SLOTS * KSLOT, 256), BF16),

time: 59.6 us -> 57.2 us (0.960)
  Pallas kernels: 57.5 us -> 55 us
    pallas_call x1, Pallas kernels: 57.5 us -> 55 us  [local(): pl.pallas_call(functools.partial(kernel, (yb, zb, xb)), out_shape=(block,...]
where the time goes in v3:
time: 57.2 us; the launch traced here: 57 us
  Pallas kernels  55 us (96%)
  local copies, waits for them, and re-layouts  1.36 us (2%)
  between operations  0.64 us (1%)
    pallas_call x1, Pallas kernels, local(): pl.pallas_call(functools.partial(kernel, (yb, zb, xb)), out_shape=(block,...  55 us
    unnamed x2, local copies, waits for them, and re-layouts  1.36 us

profile of v3, /device:TPU:1, one launch (start us, length us, event | category | flops | bytes accessed | tf_op | source)
XLA Modules:
  0.0 57.0 jit_solution(1131920856607422072)
XLA Ops:
  0.6 55.0 %two_gcr_iterations.1 = (f32[1,4,96,128]{3,2,1,0:T(8,128)S(1)}, f32[1,4,96,128]{3,2,1,0:T(8,128)S(1)}) custom-call(f32[1,4,96,128]{3,2,1,0:T(8,128)} %b_ref.1, f32[1,4,4,4608]{3,2,1,0:T(4,128)} %self_ref.1, f32[8,1,4,4,4608]{4,3,2,1,0:T(4,128)} %hop_ref.1), custom_call_target="tpu_custom_call" | custom-call | tf_op jit(solution)/shard_map/two_gcr_iterations/pallas_call | solution.py:532
  55.7 0.7 %copy.7 = f32[1,4,96,128]{3,2,1,0:T(8,128)} copy(f32[1,4,96,128]{3,2,1,0:T(8,128)S(1)} %get-tuple-element.4) | data formatting | bytes 393216
  56.3 0.7 %copy.8 = f32[1,4,96,128]{3,2,1,0:T(8,128)} copy(f32[1,4,96,128]{3,2,1,0:T(8,128)S(1)} %get-tuple-element.5) | data formatting | bytes 393216

commit v4 on v3

--- a/solution.py
+++ b/solution.py
@@ -84,12 +84,37 @@
     bottom = by_group(group, [down, up, down, jnp.zeros_like(packed)])
     work = jnp.concatenate([top, bottom], axis=0)
     row = lax.broadcasted_iota(jnp.int32, (64, 128), 0)
-    for k in range(RHS):
-        inverse = 1.0 / work[k : k + 1, k : k + 1]
-        first = work[k : k + 1, :] * inverse
-        second = work[k + 32 : k + 33, :] * inverse
-        updated = work - work[:, k : k + 1] * first - work[:, k + 32 : k + 33] * second
-        work = jnp.where(row == k, first, jnp.where(row == k + 32, second, updated))
+
+    def whole(value):
+        return jnp.broadcast_to(value, (8, 128))
+
+    for k in range(0, RHS, 2):
+        n = k + 1
+
+        def at(i, j):
+            return whole(work[i : i + 1, j : j + 1])
+
+        inverse = 1.0 / at(k, k)
+        first1 = whole(work[k : k + 1, :]) * inverse
+        first2 = whole(work[k + 32 : k + 33, :]) * inverse
+        col1, col2 = work[:, k : k + 1], work[:, k + 32 : k + 33]
+        next1 = whole(work[n : n + 1, :]) - at(n, k) * first1 - at(n, k + 32) * first2
+        next2 = whole(work[n + 32 : n + 33, :]) - at(n + 32, k) * first1 - at(n + 32, k + 32) * first2
+        drop = at(n, k) * at(k, n) + at(n, k + 32) * at(k + 32, n)
+        inverse2 = 1.0 / (at(n, n) - drop * inverse)
+        second1, second2 = next1 * inverse2, next2 * inverse2
+        up11, up21 = at(k, n) * inverse, at(k + 32, n) * inverse
+        up12, up22 = at(k, n + 32) * inverse, at(k + 32, n + 32) * inverse
+        later1 = work[:, n : n + 1] - col1 * up11[0:1] - col2 * up21[0:1]
+        later2 = work[:, n + 32 : n + 33] - col1 * up12[0:1] - col2 * up22[0:1]
+        updated = work - col1 * first1[0:1] - col2 * first2[0:1] - later1 * second1[0:1] - later2 * second2[0:1]
+        first1, first2 = (
+            first1 - up11 * second1 - up12 * second2,
+            first2 - up21 * second1 - up22 * second2,
+        )
+        for place, value in ((k, first1), (k + 32, first2), (n, second1), (n + 32, second2)):
+            updated = jnp.where(row == place, value[0:1], updated)
+        work = updated
     return work
 
 
@@ -125,6 +150,7 @@
     halo,
     acc,
     second,
+    pieces,
     pay,
     rs_buf,
     y_buf,
@@ -452,8 +478,28 @@
     def form_of(column):
         return real_form(column[:32], column[32:])
 
+    def split(values):
+        hi = values.astype(BF16)
+        return hi, (values - hi.astype(F32)).astype(BF16)
+
+    def keep_pieces(index, ref, first):
+        rows = field_rows(ref, first)
+        hi, lo = split(jnp.concatenate([rows, field_j(rows)], axis=1))
+        pieces[index, 0] = hi
+        pieces[index, 1] = lo
+
+    def combined(index, coef):
+        hi, lo = split(coef)
+        field_hi = pieces[index, 0]
+        out = jnp.dot(field_hi, hi, preferred_element_type=F32)
+        out = out + jnp.dot(pieces[index, 1], hi, preferred_element_type=F32)
+        return out + jnp.dot(field_hi, lo, preferred_element_type=F32)
+
     red1[2]()
     red2[1]()
+    keep_pieces(0, ext.at[0], 1)
+    keep_pieces(1, ext.at[1], 1)
+    keep_pieces(2, second, 0)
     red1[3]()
     red2[2]()
     gram = red1[4]()[0:32]
@@ -493,16 +539,10 @@
     follow = dot(jnp.concatenate([form_of(keep), coef1_form], axis=0)[:, 0:64], solved2)
     step_a = column_matrix(pltpu.roll(coef1, 64, 1) + follow[:64], 2)
     step_e = column_matrix(follow[64:], 2)
-    rhs_rows = field_rows(ext.at[0], 1)
-    rhs_pair = jnp.concatenate([rhs_rows, field_j(rhs_rows)], axis=1)
-    image_rows = field_rows(ext.at[1], 1)
-    image_pair = jnp.concatenate([image_rows, field_j(image_rows)], axis=1)
-    twice_rows = field_rows(second)
-    twice_pair = jnp.concatenate([twice_rows, field_j(twice_rows)], axis=1)
-    answer = dot(jnp.concatenate([rhs_pair, image_pair], axis=1), jnp.concatenate([step_a, -step_e], axis=0))
-    sol_ref[0] = answer.reshape(ROWS, 2 * NV, 128)
-    change = dot(jnp.concatenate([image_pair, twice_pair], axis=1), jnp.concatenate([-step_a, step_e], axis=0))
-    res_ref[0] = (rhs_rows + change).reshape(ROWS, 2 * NV, 128)
+    from_image = combined(1, jnp.concatenate([-step_e, -step_a], axis=1))
+    sol_ref[0] = (combined(0, step_a) + from_image[:, 0:128]).reshape(ROWS, 2 * NV, 128)
+    change = combined(2, step_e) + from_image[:, 128:256]
+    res_ref[0] = (field_rows(ext.at[0], 1) + change).reshape(ROWS, 2 * NV, 128)
 
     for which in range(2):
         t_copy(which, 0).wait_send()
@@ -544,6 +584,7 @@
                 pltpu.VMEM((2, 4, ROWS, 2 * NV, 128), F32),
                 pltpu.VMEM((ROWS, 96, 256), F32),
                 pltpu.VMEM((ROWS, 2 * NV, 128), F32),
+                pltpu.VMEM((3, 2, ROWS * 2 * NV, 256), BF16),
                 pltpu.VMEM((2, xb, piece, 128), F32),
                 pltpu.VMEM((2, xb, piece, 128), F32),
                 pltpu.VMEM((2, yb, piece, 128), F32),

time: 57.2 us -> 56.2 us (0.983)
  Pallas kernels: 55 us -> 54.1 us
    pallas_call x1, Pallas kernels: 55 us -> 54.1 us  [local(): pl.pallas_call(functools.partial(kernel, (yb, zb, xb)), out_shape=(block,...]
where the time goes in v4:
time: 56.2 us; the launch traced here: 56.1 us
  Pallas kernels  54.1 us (96%)
  local copies, waits for them, and re-layouts  1.36 us (2%)
  between operations  0.64 us (1%)
    pallas_call x1, Pallas kernels, local(): pl.pallas_call(functools.partial(kernel, (yb, zb, xb)), out_shape=(block,...  54.1 us
    unnamed x2, local copies, waits for them, and re-layouts  1.36 us

profile of v4, /device:TPU:1, one launch (start us, length us, event | category | flops | bytes accessed | tf_op | source)
XLA Modules:
  0.0 56.1 jit_solution(7713945975974776565)
XLA Ops:
  0.6 54.1 %two_gcr_iterations.1 = (f32[1,4,96,128]{3,2,1,0:T(8,128)S(1)}, f32[1,4,96,128]{3,2,1,0:T(8,128)S(1)}) custom-call(f32[1,4,96,128]{3,2,1,0:T(8,128)} %b_ref.1, f32[1,4,4,4608]{3,2,1,0:T(4,128)} %self_ref.1, f32[8,1,4,4,4608]{4,3,2,1,0:T(4,128)} %hop_ref.1), custom_call_target="tpu_custom_call" | custom-call | tf_op jit(solution)/shard_map/two_gcr_iterations/pallas_call | solution.py:572
  54.7 0.7 %copy.7 = f32[1,4,96,128]{3,2,1,0:T(8,128)} copy(f32[1,4,96,128]{3,2,1,0:T(8,128)S(1)} %get-tuple-element.4) | data formatting | bytes 393216
  55.4 0.7 %copy.8 = f32[1,4,96,128]{3,2,1,0:T(8,128)} copy(f32[1,4,96,128]{3,2,1,0:T(8,128)S(1)} %get-tuple-element.5) | data formatting | bytes 393216

commit v5 on v4

--- a/solution.py
+++ b/solution.py
@@ -457,12 +457,10 @@
     image_pair = jnp.concatenate([image_rows, field_j(image_rows)], axis=1)
     twice_rows = field_rows(second)
     twice_pair = jnp.concatenate([twice_rows, field_j(twice_rows)], axis=1)
-    with_image = dot(image_rows.T, twice_pair)
     with_twice = dot(twice_rows.T, jnp.concatenate([image_pair, twice_pair, rhs_pair], axis=1))
-    with_both = jnp.concatenate([with_image, with_twice[:, 0:256]], axis=1)
     red2[0](
         jnp.concatenate(
-            [packed_inner(with_both, (0, 1, 2, 3)), packed_inner(with_twice, (2, 3, 4, 5))], axis=0
+            [packed_inner(with_twice, (0, 1)), packed_inner(with_twice, (2, 3, 4, 5))], axis=0
         )
     )
 
@@ -514,7 +512,8 @@
     reduced = red2[4]()
     upper, lower = reduced[:32], reduced[32:]
 
-    cross_form = form_of(stacked(upper, 0))
+    adjoint_form = form_of(stacked(upper, 0))
+    cross_form = jnp.concatenate([adjoint_form, jnp.zeros_like(adjoint_form)], axis=0).T[0:64]
     image_part = gram_column - dot(cross_form[:, 0:64], coef1)
     projection = dot(inverse_form[:, 0:64], image_part)
     row64 = lax.broadcasted_iota(jnp.int32, (64, 128), 0)
@@ -524,7 +523,7 @@
     grams = jnp.concatenate(
         [
             gram_form + pltpu.roll(cross_form, 64, 1),
-            form_of(stacked(upper, 2)) + pltpu.roll(form_of(stacked(lower, 0)), 64, 1),
+            adjoint_form + pltpu.roll(form_of(stacked(lower, 0)), 64, 1),
         ],
         axis=0,
     )

time: 56.2 us -> 56.2 us (level)
  no operation moved by 1% of the time
where the time goes in v5:
time: 56.2 us; the launch traced here: 56.1 us
  Pallas kernels  54.1 us (96%)
  local copies, waits for them, and re-layouts  1.36 us (2%)
  between operations  0.64 us (1%)
    pallas_call x1, Pallas kernels, local(): pl.pallas_call(functools.partial(kernel, (yb, zb, xb)), out_shape=(block,...  54.1 us
    unnamed x2, local copies, waits for them, and re-layouts  1.36 us

profile of v5, /device:TPU:1, one launch (start us, length us, event | category | flops | bytes accessed | tf_op | source)
XLA Modules:
  0.0 56.1 jit_solution(12786239281570537735)
XLA Ops:
  0.6 54.1 %two_gcr_iterations.1 = (f32[1,4,96,128]{3,2,1,0:T(8,128)S(1)}, f32[1,4,96,128]{3,2,1,0:T(8,128)S(1)}) custom-call(f32[1,4,96,128]{3,2,1,0:T(8,128)} %b_ref.1, f32[1,4,4,4608]{3,2,1,0:T(4,128)} %self_ref.1, f32[8,1,4,4,4608]{4,3,2,1,0:T(4,128)} %hop_ref.1), custom_call_target="tpu_custom_call" | custom-call | tf_op jit(solution)/shard_map/two_gcr_iterations/pallas_call | solution.py:571
  54.7 0.7 %copy.7 = f32[1,4,96,128]{3,2,1,0:T(8,128)} copy(f32[1,4,96,128]{3,2,1,0:T(8,128)S(1)} %get-tuple-element.4) | data formatting | bytes 393216
  55.4 0.7 %copy.8 = f32[1,4,96,128]{3,2,1,0:T(8,128)} copy(f32[1,4,96,128]{3,2,1,0:T(8,128)S(1)} %get-tuple-element.5) | data formatting | bytes 393216
